TPU v7x, 32 devices: a whole 2x2x4 slice. The times are simulated.
32 devices in a mesh: pipe: 4 (over y, core), expert: 4 (over z), tensor: 2 (over x).
Axes of the slice: x: 2, y: 2, z: 4, core: 2. Of those that a mesh axis runs over, the one named last changes fastest.
Arguments:
- sent_grad: bfloat16 [4, 512, 3584], P('pipe', 'expert', 'tensor'), may hold values from -4 to 4
- head_grad: bfloat16 [512, 3584], P('expert', 'tensor'), may hold values from -4 to 4
- probs: bfloat16 [4, 512, 8], P('pipe', 'expert'), may hold values from 0.049804688 to 1
- expert_ids: int32 [4, 512, 8], P('pipe', 'expert'), may hold values from 0 to 63, as said below
- hidden_act: bfloat16 [4, 64, 68, 1024], P('pipe', 'expert', None, 'tensor'), may hold values from -0.75 to 0.75
Outputs:
- w_down_grad: bfloat16 [4, 64, 1024, 3584], P('pipe', 'expert', 'tensor')
Inputs may be any that keep to these rules, and one draw needn't show every extreme that they name: `expert_ids`: each token names 8 different experts. In each section and each block of 128 tokens one expert is named by exactly 17 pairs, one by 17 - 2 pairs, and every other expert by 17 - 1 pairs.
All inputs are finite; a program needn't handle non-finite values.
Results may differ from a plain program's by a relative error of at most 0.0049.
Values may be sent and summed in bfloat16 or wider, within the bound.
No kernel may reach another device: no remote copies, remote signals or barrier semaphores. Data moves between devices by JAX's collectives and lax.ppermute only.
A program may use at most 192 MiB of HBM per device.

v0:
```python
import functools
import itertools

import jax
import jax.numpy as jnp
from jax import lax
from jax.experimental import pallas as pl
from jax.experimental.pallas import tpu as pltpu
from jax.sharding import PartitionSpec as P

EXPERTS = 64
TOPK = 8
TOK = 128
MOST = 17
ROOM = 32
BUFFERS = 4


def passed_along(array, axis, by):
    peers = lax.axis_size(axis)
    pairs = [(i, i + by) for i in range(peers) if 0 <= i + by < peers]
    return lax.ppermute(array, axis, pairs)


def slot_ranks(pair_ids):
    onehot = (pair_ids[:, :, None] == jnp.arange(EXPERTS, dtype=jnp.int32)[None, None, :]).astype(
        jnp.int32
    )
    before = jnp.cumsum(onehot, axis=1) - onehot
    return jnp.sum(before * onehot, axis=2)


def place_rows(targets, capacity, source_rows, gate_values):
    pair_count = targets.shape[0]
    owner_pair = (
        jnp.full((capacity,), pair_count, jnp.int32)
        .at[targets]
        .set(jnp.arange(pair_count, dtype=jnp.int32), mode="drop")
    )
    filled = owner_pair < pair_count
    safe_pair = jnp.minimum(owner_pair, pair_count - 1)
    placed = jnp.where(
        filled[:, None], source_rows[safe_pair // TOPK], jnp.zeros((), source_rows.dtype)
    )
    placed_gate = jnp.where(
        filled, gate_values.reshape(-1)[safe_pair], jnp.zeros((), gate_values.dtype)
    )
    return (placed, placed_gate)


def arriving(sent_grad, head_grad):
    shifted = passed_along(sent_grad, "pipe", -1)
    is_last = lax.axis_index("pipe") == lax.axis_size("pipe") - 1
    return jnp.where(is_last, head_grad, shifted[0])


def local_by_slots(sent_grad, head_grad, probs, expert_ids, hidden_act):
    incoming = arriving(sent_grad, head_grad)
    feat_dev = incoming.shape[1]
    local_ids = expert_ids[0].reshape(1, TOK * TOPK)
    local_targets = (local_ids * MOST + slot_ranks(local_ids)).reshape(-1)
    send_rows, send_gate = place_rows(local_targets, EXPERTS * MOST, incoming, probs[0])
    recv_rows, recv_gate = (
        lax.all_to_all(
            send_rows.reshape(EXPERTS, MOST, feat_dev),
            "expert",
            split_axis=0,
            concat_axis=1,
            tiled=True,
        ),
        lax.all_to_all(
            send_gate.reshape(EXPERTS, MOST), "expert", split_axis=0, concat_axis=1, tiled=True
        ),
    )
    gate_wide = recv_gate.astype(jnp.float32)[:, :, None]
    full_rows = lax.all_gather(recv_rows, "tensor", axis=2, tiled=True)
    weighted = (full_rows.astype(jnp.float32) * gate_wide).astype(jnp.bfloat16)
    weight_grad = jnp.einsum(
        "esh,esd->ehd", hidden_act[0], weighted, preferred_element_type=jnp.float32
    ).astype(jnp.bfloat16)
    return weight_grad[None]


def notes_kernel(ids_ref, probs_ref, notes_ref):
    notes_ref[...] = jnp.concatenate(
        [ids_ref[...].astype(jnp.float32), probs_ref[...].astype(jnp.float32)], axis=0
    ).astype(jnp.bfloat16)


def turn_kernel(n_expert, act_ref, turned_ref):
    owned, slot_count, _ = act_ref.shape
    me = lax.axis_index("expert")
    slot = lax.broadcasted_iota(jnp.int32, (slot_count, n_expert * ROOM), 0)
    spot = lax.broadcasted_iota(jnp.int32, (slot_count, n_expert * ROOM), 1)
    block = jnp.zeros_like(slot)
    for b in range(1, n_expert):
        block += (slot >= b * MOST).astype(jnp.int32)
    back = me - block
    back = jnp.where(back < 0, back + n_expert, back)
    target = back * ROOM + slot - block * MOST
    for e in range(owned):
        turned_ref[e] = lax.dot_general(
            act_ref[e],
            (spot == target + e).astype(jnp.bfloat16),
            (((0,), (0,)), ((), ())),
            preferred_element_type=jnp.float32,
        ).astype(jnp.bfloat16)


def place_kernel(owned, *refs):
    *notes, place_ref = refs
    first = lax.axis_index("expert") * owned
    rows = place_ref.shape[1]
    experts = (first + lax.broadcasted_iota(jnp.int32, (owned, TOK), 0)).astype(jnp.float32)
    earlier = (
        lax.broadcasted_iota(jnp.int32, (TOK, TOK), 0)
        < lax.broadcasted_iota(jnp.int32, (TOK, TOK), 1)
    ).astype(jnp.float32)
    row = lax.broadcasted_iota(jnp.int32, (rows, owned), 0)
    start = lax.broadcasted_iota(jnp.int32, (rows, owned), 1) * MOST
    spread = ((row >= start) & (row < start + MOST)).astype(jnp.float32)
    wanted = lax.broadcasted_iota(jnp.int32, (rows, TOK), 0)
    for e in range(1, owned):
        wanted -= MOST * (
            lax.broadcasted_iota(jnp.int32, (rows, TOK), 0) >= e * MOST
        ).astype(jnp.int32)
    wanted = wanted.astype(jnp.float32)
    for k, note in enumerate(notes):
        meta = note[...].astype(jnp.float32)
        named = jnp.zeros((owned, TOK), jnp.float32)
        gate = jnp.zeros((owned, TOK), jnp.float32)
        for c in range(TOPK):
            hit = experts == meta[c : c + 1, :]
            named = jnp.where(hit, 1.0, named)
            gate = jnp.where(hit, meta[TOPK + c : TOPK + c + 1, :], gate)
        rank = jnp.dot(named, earlier, preferred_element_type=jnp.float32)
        rank = jnp.where(named > 0.0, rank, -1.0)
        rank = jnp.dot(spread, rank, preferred_element_type=jnp.float32)
        gate = jnp.dot(spread, gate, preferred_element_type=jnp.float32)
        place_ref[k] = jnp.where(rank == wanted, gate, 0.0).astype(jnp.bfloat16)


def early_kernel(ks, place_ref, *refs):
    blocks, outs = refs[: len(ks)], refs[len(ks) :]
    weigh_tiles([place_ref.at[k] for k in ks], blocks, outs)


def weigh_tiles(places, blocks, outs):
    half = blocks[0].shape[1] // 2

    @pl.loop(0, 2)
    def _(t):
        wide = pl.ds(pl.multiple_of(t * half, half), half)
        for place, block, out in zip(places, blocks, outs):
            out[:, wide] = jnp.dot(
                place[...], block[:, wide], preferred_element_type=jnp.float32
            ).astype(jnp.bfloat16)


def grad_kernel(n_expert, other, early, place_ref, act_ref, *refs):
    blocks = refs[:n_expert]
    out_ref, weighted_ref, done_ref, out_sem = refs[-4:]
    owned, hid, _ = act_ref.shape
    features = done_ref.shape[2]
    side = lax.rem(lax.axis_index("tensor") + other, lax.axis_size("tensor"))
    column = pl.multiple_of(side * features, 128)

    def leave(e):
        slot = lax.rem(e, BUFFERS)
        return pltpu.make_async_copy(
            done_ref.at[slot], out_ref.at[e, :, pl.ds(column, features)], out_sem.at[slot]
        )

    late = [k for k in range(n_expert) if k not in early]
    weighted = list(blocks)
    for i, k in enumerate(late):
        weighted[k] = weighted_ref.at[i]
    weigh_tiles([place_ref.at[k] for k in late], [blocks[k] for k in late], [weighted[k] for k in late])

    @pl.loop(0, owned)
    def _(e):
        @pl.when(e >= BUFFERS)
        def _():
            leave(e - BUFFERS).wait()

        window = pl.ds(pl.multiple_of(e * 16, 16), ROOM)
        for n in range(0, features, 256):
            wide = slice(n, min(n + 256, features))
            right = jnp.concatenate([rows[window, wide] for rows in weighted], axis=0)
            done_ref[lax.rem(e, BUFFERS), :, wide] = jnp.dot(
                act_ref[e], right, preferred_element_type=jnp.float32
            ).astype(jnp.bfloat16)
        leave(e).start()

    @pl.loop(owned - BUFFERS, owned)
    def _(e):
        leave(e).wait()


def local_by_tokens(sent_grad, head_grad, probs, expert_ids, hidden_act):
    n_expert = lax.axis_size("expert")
    n_tensor = lax.axis_size("tensor")
    owned, _, hid = hidden_act.shape[1:]
    feat_dev = sent_grad.shape[2]
    vmem = pl.BlockSpec(memory_space=pltpu.VMEM)
    anywhere = pl.BlockSpec(memory_space=pl.ANY)

    def small_call(kernel, shapes, operands, name):
        return pl.pallas_call(
            kernel,
            out_shape=[jax.ShapeDtypeStruct(shape, jnp.bfloat16) for shape in shapes],
            in_specs=[vmem] * len(operands),
            out_specs=[vmem] * len(shapes),
            compiler_params=pltpu.CompilerParams(vmem_limit_bytes=16 * 2**20),
            name=name,
        )(*operands)

    def turned(array, pipe=0, expert=0, tensor=0):
        axes = ("pipe", "expert", "tensor")
        sizes = [lax.axis_size(axis) for axis in axes]
        steps = (pipe, expert, tensor)

        def rank(place):
            return (place[0] * sizes[1] + place[1]) * sizes[2] + place[2]

        pairs = []
        for place in itertools.product(*map(range, sizes)):
            target = [(i + by) % size for i, by, size in zip(place, steps, sizes)]
            pairs.append((rank(place), rank(target)))
        return lax.ppermute(array, axes, pairs)

    def grad_into(out, blocks, other, early):
        operands = [place, act, *blocks]
        in_specs = [vmem] * len(operands)
        aliases = {}
        if out is not None:
            aliases = {len(operands): 0}
            in_specs.append(anywhere)
            operands.append(out)
        return pl.pallas_call(
            functools.partial(grad_kernel, n_expert, other, early),
            out_shape=jax.ShapeDtypeStruct((owned, hid, n_tensor * feat_dev), jnp.bfloat16),
            in_specs=in_specs,
            out_specs=anywhere,
            scratch_shapes=[
                pltpu.VMEM((n_expert - len(early), place.shape[1], feat_dev), jnp.bfloat16),
                pltpu.VMEM((BUFFERS, hid, feat_dev), jnp.bfloat16),
                pltpu.SemaphoreType.DMA((BUFFERS,)),
            ],
            input_output_aliases=aliases,
            compiler_params=pltpu.CompilerParams(vmem_limit_bytes=28 * 2**20),
            cost_estimate=pl.CostEstimate(
                flops=2 * owned * hid * 256 * feat_dev,
                bytes_accessed=2 * owned * hid * feat_dev,
                transcendentals=0,
            ),
            name="weight_grad",
        )(*operands)

    payload = jnp.where(lax.axis_index("pipe") == 0, head_grad, sent_grad[0])
    blocks = {1: turned(payload, -1, 1)}
    beside = {0: {t: turned(payload, -1, 0, t) for t in range(1, n_tensor)}}
    (notes,) = small_call(
        notes_kernel, [(2 * TOPK, TOK)], [expert_ids[0].T, probs[0].T], "notes"
    )
    notes = [notes] + [turned(notes, 0, k) for k in range(1, n_expert)]
    (act,) = small_call(
        functools.partial(turn_kernel, n_expert),
        [(owned, hid, n_expert * ROOM)],
        [hidden_act[0]],
        "turn",
    )
    beside[0], payload, act, notes[1:] = lax.optimization_barrier(
        (beside[0], payload, act, notes[1:])
    )
    blocks[n_expert - 1] = turned(payload, -1, -1)
    for k in range(2, n_expert - 1):
        blocks[k] = turned(blocks[k - 1], 0, 1)
    (place,) = small_call(
        functools.partial(place_kernel, owned), [(n_expert, 16 * (owned + 1), TOK)], notes, "place"
    )
    blocks[0] = turned(payload, -1)

    def weighed(sources, ks):
        done = small_call(
            functools.partial(early_kernel, ks),
            [(place.shape[1], feat_dev)] * len(ks),
            [place, *(sources[k] for k in ks)],
            "early",
        )
        return dict(zip(ks, done))

    last = n_expert - 1
    early = tuple(range(1, last))
    own = weighed(blocks, early)
    for k in range(1, n_expert):
        if k == last - 1:
            blocks[k], own, beside[k - 1] = lax.optimization_barrier((blocks[k], own, beside[k - 1]))
        beside[k] = {t: turned(blocks[k], 0, 0, t) for t in range(1, n_tensor)}
    out = grad_into(None, [own.get(k, blocks[k]) for k in range(n_expert)], 0, early)
    for t in range(1, n_tensor):
        out = grad_into(out, [beside[k][t] for k in range(n_expert)], n_tensor - t, ())
    return out[None]


def local(*arrays):
    owned, slot_count = arrays[4].shape[1:3]
    tokens = lax.axis_size("expert") * TOK
    by_tokens = owned <= 16 and tokens <= owned * slot_count
    return (local_by_tokens if by_tokens else local_by_slots)(*arrays)


def solution(mesh):
    in_specs = (
        P("pipe", "expert", "tensor"),
        P("expert", "tensor"),
        P("pipe", "expert", None),
        P("pipe", "expert", None),
        P("pipe", "expert", None, "tensor"),
    )
    out_specs = P("pipe", "expert", "tensor", None)
    return jax.shard_map(local, mesh=mesh, in_specs=in_specs, out_specs=out_specs, check_vma=False)
```

profile of v0, /device:TPU:0, one launch (start us, length us, event | category | flops | bytes accessed | tf_op | source)
XLA Modules:
  0.0 67.4 jit_solution(16648722541016443714)
XLA Ops:
  0.0 0.0 copy-start.2
  0.0 1.3 %bitcast_select_fusion = bf16[128,1792]{1,0:T(8,128)(2,1)S(1)} fusion(bf16[128,1792]{1,0:T(8,128)(2,1)} %param.6, bf16[1,128,1792]{2,1,0:T(8,128)(2,1)} %param.5, pred[]{:T(512)S(6)} %eq.3), kind=kLoop, calls=%fused_computation.1 | loop fusion | flops 229376 | bytes 1376257 | tf_op jit(solution)/shard_map/jit(_where)/select_n | solution.py:260
  1.3 3.3 %collective-permute-start.4 = (bf16[128,1792]{1,0:T(8,128)(2,1)S(1)}, bf16[128,1792]{1,0:T(8,128)(2,1)S(1)}, u32[]{:S(2)}, u32[]{:S(2)}) collective-permute-start(bf16[128,1792]{1,0:T(8,128)(2,1)S(1)} %bitcast_select_fusion), channel_id=1, source_target_pairs={{0,26},{1,27},{2,28},{3,29},{4,30},{5,31},{6,24},{7,25},{8,2},{9,3... | collective-permute-start | bytes 1376264 | tf_op jit(solution)/shard_map/ppermute | solution.py:230
  4.6 1.8 %collective-permute-start = (bf16[128,1792]{1,0:T(8,128)(2,1)S(1)}, bf16[128,1792]{1,0:T(8,128)(2,1)S(1)}, u32[]{:S(2)}, u32[]{:S(2)}) collective-permute-start(bf16[128,1792]{1,0:T(8,128)(2,1)S(1)} %bitcast_select_fusion), channel_id=1, source_target_pairs={{0,25},{1,24},{2,27},{3,26},{4,29},{5,28},{6,31},{7,30},{8,1},{9,0... | collective-permute-start | bytes 1376264 | tf_op jit(solution)/shard_map/ppermute | solution.py:230
  6.4 0.0 copy-start
  6.4 0.7 %copy-done = s32[1,128,8]{1,2,0:T(8,128)S(1)} copy-done((s32[1,128,8]{1,2,0:T(8,128)S(1)}, s32[1,128,8]{1,2,0:T(8,128)}, u32[]{:S(2)}) %copy-start) | copy-done | bytes 4120
  7.1 0.0 copy-start.1
  7.1 0.7 %copy-done.1 = bf16[1,128,8]{1,2,0:T(8,128)(2,1)S(1)} copy-done((bf16[1,128,8]{1,2,0:T(8,128)(2,1)S(1)}, bf16[1,128,8]{1,2,0:T(8,128)(2,1)}, u32[]{:S(2)}) %copy-start.1) | copy-done | bytes 2072
  7.8 2.2 %collective-permute-start.3 = (bf16[16,128]{1,0:T(8,128)(2,1)S(1)}, bf16[16,128]{1,0:T(8,128)(2,1)S(1)}, u32[]{:S(2)}, u32[]{:S(2)}) collective-permute-start(bf16[16,128]{1,0:T(8,128)(2,1)S(1)} %notes.1.refs_0_), channel_id=1, source_target_pairs={{0,6},{1,7},{2,0},{3,1},{4,2},{5,3},{6,4},{7,5},{8,14},{9,15},{10,... | collective-permute-start | bytes 12296 | tf_op jit(solution)/shard_map/ppermute | solution.py:230
  10.0 0.8 %collective-permute-start.2 = (bf16[16,128]{1,0:T(8,128)(2,1)S(1)}, bf16[16,128]{1,0:T(8,128)(2,1)S(1)}, u32[]{:S(2)}, u32[]{:S(2)}) collective-permute-start(bf16[16,128]{1,0:T(8,128)(2,1)S(1)} %notes.1.refs_0_), channel_id=1, source_target_pairs={{0,4},{1,5},{2,6},{3,7},{4,0},{5,1},{6,2},{7,3},{8,12},{9,13},{10,... | collective-permute-start | bytes 12296 | tf_op jit(solution)/shard_map/ppermute | solution.py:230
  10.8 1.6 %collective-permute-start.1 = (bf16[16,128]{1,0:T(8,128)(2,1)S(1)}, bf16[16,128]{1,0:T(8,128)(2,1)S(1)}, u32[]{:S(2)}, u32[]{:S(2)}) collective-permute-start(bf16[16,128]{1,0:T(8,128)(2,1)S(1)} %notes.1.refs_0_), channel_id=1, source_target_pairs={{0,2},{1,3},{2,4},{3,5},{4,6},{5,7},{6,0},{7,1},{8,10},{9,11},{10,... | collective-permute-start | bytes 12296 | tf_op jit(solution)/shard_map/ppermute | solution.py:230
  12.4 0.0 copy-done.2
  12.4 0.6 copy.9
  13.0 0.8 %turn.1.act_ref = bf16[16,512,128]{2,1,0:T(8,128)(2,1)S(1)} custom-call(bf16[16,68,512]{2,1,0:T(8,128)(2,1)S(1)} %bitcast.12), custom_call_target="tpu_custom_call" | custom-call | tf_op jit(solution)/shard_map/turn/pallas_call | solution.py:209
  13.8 1.6 %collective-permute-done.4.refs_0_ = bf16[128,1792]{1,0:T(8,128)(2,1)S(1)} collective-permute-done((bf16[128,1792]{1,0:T(8,128)(2,1)S(1)}, bf16[128,1792]{1,0:T(8,128)(2,1)S(1)}, u32[]{:S(2)}, u32[]{:S(2)}) %collective-permute-start.4) | collective-permute-done | bytes 458784 | tf_op jit(solution)/shard_map/ppermute | solution.py:230
  15.3 1.2 %collective-permute-start.5 = (bf16[128,1792]{1,0:T(8,128)(2,1)S(1)}, bf16[128,1792]{1,0:T(8,128)(2,1)S(1)}, u32[]{:S(2)}, u32[]{:S(2)}) collective-permute-start(bf16[128,1792]{1,0:T(8,128)(2,1)S(1)} %collective-permute-done.4.refs_0_), channel_id=1, source_target_pairs={{0,2},{1,3},{2,4},{3,5},{4,6},{5,7},{6,0},{7,1},{8,10},{9,11},{10,... | collective-permute-start | bytes 1376264 | tf_op jit(solution)/shard_map/ppermute | solution.py:230
  16.5 0.0 collective-permute-done.3.refs_3_
  16.5 1.7 %collective-permute-start.6 = (bf16[128,1792]{1,0:T(8,128)(2,1)S(1)}, bf16[128,1792]{1,0:T(8,128)(2,1)S(1)}, u32[]{:S(2)}, u32[]{:S(2)}) collective-permute-start(bf16[128,1792]{1,0:T(8,128)(2,1)S(1)} %collective-permute-done.4.refs_0_), channel_id=1, source_target_pairs={{0,1},{1,0},{2,3},{3,2},{4,5},{5,4},{6,7},{7,6},{8,9},{9,8},{10,11... | collective-permute-start | bytes 1376264 | tf_op jit(solution)/shard_map/ppermute | solution.py:230
  18.2 0.0 collective-permute-done.2.refs_2_
  18.2 0.0 collective-permute-done.1.refs_1_
  18.2 0.0 collective-permute-done.refs_0_
  18.2 5.2 %collective-permute-start.8 = (bf16[128,1792]{1,0:T(8,128)(2,1)S(1)}, bf16[128,1792]{1,0:T(8,128)(2,1)S(1)}, u32[]{:S(2)}, u32[]{:S(2)}) collective-permute-start(bf16[128,1792]{1,0:T(8,128)(2,1)S(1)} %bitcast_select_fusion), channel_id=1, source_target_pairs={{0,30},{1,31},{2,24},{3,25},{4,26},{5,27},{6,28},{7,29},{8,6},{9,7... | collective-permute-start | bytes 1376264 | tf_op jit(solution)/shard_map/ppermute | solution.py:230
  23.5 0.3 collective-permute-start.10
  23.7 0.7 %place.1.place_ref = bf16[4,272,128]{2,1,0:T(8,128)(2,1)S(1)} custom-call(bf16[16,128]{1,0:T(8,128)(2,1)S(1)} %notes.1.refs_0_, bf16[16,128]{1,0:T(8,128)(2,1)S(1)} %collective-permute-done.1.refs_1_, bf16[16,128]{1,0:T(8,128)(2,1)S(1)} %collective-permute-done.2.refs_2_, bf16[16,128]{1,0:T(8,128)(2,1)S(1)} %collective-permute-done.3.refs_3_), custom_call_target="tpu_custom_call" | custom-call | tf_op jit(solution)/shard_map/place/pallas_call | solution.py:209
  24.5 4.1 %collective-permute-done.5.refs_1_ = bf16[128,1792]{1,0:T(8,128)(2,1)S(1)} collective-permute-done((bf16[128,1792]{1,0:T(8,128)(2,1)S(1)}, bf16[128,1792]{1,0:T(8,128)(2,1)S(1)}, u32[]{:S(2)}, u32[]{:S(2)}) %collective-permute-start.5) | collective-permute-done | bytes 458784 | tf_op jit(solution)/shard_map/ppermute | solution.py:230
  28.6 0.9 %early.1 = (bf16[272,1792]{1,0:T(8,128)(2,1)S(1)}, bf16[272,1792]{1,0:T(8,128)(2,1)S(1)}) custom-call(bf16[4,272,128]{2,1,0:T(8,128)(2,1)S(1)} %place.1.place_ref, bf16[128,1792]{1,0:T(8,128)(2,1)S(1)} %collective-permute-done.4.refs_0_, bf16[128,1792]{1,0:T(8,128)(2,1)S(1)} %collective-permute-done.5.refs_1_), custom_call_target="tpu_custom_call" | custom-call | tf_op jit(solution)/shard_map/early/pallas_call | solution.py:209
  29.5 0.0 collective-permute-done.6.refs_1_
  29.5 4.4 %collective-permute-start.7 = (bf16[128,1792]{1,0:T(8,128)(2,1)S(1)}, bf16[128,1792]{1,0:T(8,128)(2,1)S(1)}, u32[]{:S(2)}, u32[]{:S(2)}) collective-permute-start(bf16[128,1792]{1,0:T(8,128)(2,1)S(1)} %collective-permute-done.5.refs_1_), channel_id=1, source_target_pairs={{0,1},{1,0},{2,3},{3,2},{4,5},{5,4},{6,7},{7,6},{8,9},{9,8},{10,11... | collective-permute-start | bytes 1376264 | tf_op jit(solution)/shard_map/ppermute | solution.py:230
  33.9 6.3 %collective-permute-done.8.refs_3_ = bf16[128,1792]{1,0:T(8,128)(2,1)S(1)} collective-permute-done((bf16[128,1792]{1,0:T(8,128)(2,1)S(1)}, bf16[128,1792]{1,0:T(8,128)(2,1)S(1)}, u32[]{:S(2)}, u32[]{:S(2)}) %collective-permute-start.8) | collective-permute-done | bytes 458784 | tf_op jit(solution)/shard_map/ppermute | solution.py:230
  40.2 0.2 collective-permute-start.9
  40.4 0.0 collective-permute-done.10.refs_0_
  40.4 12.2 %weight_grad.2.refs_4_ = bf16[16,512,3584]{2,1,0:T(8,128)(2,1)} custom-call(bf16[4,272,128]{2,1,0:T(8,128)(2,1)S(1)} %place.1.place_ref, bf16[16,512,128]{2,1,0:T(8,128)(2,1)S(1)} %turn.1.act_ref, bf16[128,1792]{1,0:T(8,128)(2,1)S(1)} %collective-permute-done.10.refs_0_, bf16[272,1792]{1,0:T(8,128)(2,1)S(1)} %get-tuple-element.27.refs_1_, ...), custom_call_target="tpu_custom_call" | custom-call | flops 7516192768 | bytes 29360128 | tf_op jit(solution)/shard_map/weight_grad/pallas_call | solution.py:240
  52.6 2.0 %collective-permute-done.9.refs_3_ = bf16[128,1792]{1,0:T(8,128)(2,1)S(1)} collective-permute-done((bf16[128,1792]{1,0:T(8,128)(2,1)S(1)}, bf16[128,1792]{1,0:T(8,128)(2,1)S(1)}, u32[]{:S(2)}, u32[]{:S(2)}) %collective-permute-start.9) | collective-permute-done | bytes 458784 | tf_op jit(solution)/shard_map/ppermute | solution.py:230
  54.6 0.0 collective-permute-done.7.refs_2_
  54.6 12.8 %weight_grad.3 = bf16[16,512,3584]{2,1,0:T(8,128)(2,1)} custom-call(bf16[4,272,128]{2,1,0:T(8,128)(2,1)S(1)} %place.1.place_ref, bf16[16,512,128]{2,1,0:T(8,128)(2,1)S(1)} %turn.1.act_ref, bf16[128,1792]{1,0:T(8,128)(2,1)S(1)} %collective-permute-done.refs_0_, bf16[128,1792]{1,0:T(8,128)(2,1)S(1)} %collective-permute-done.6.refs_1_, ...), custom_call_target="tpu_custom_call", output_to_operand_aliasing={{}: (6, {})} | custom-call | flops 7516192768 | bytes 29360128 | tf_op jit(solution)/shard_map/weight_grad/pallas_call | solution.py:240
  (1 shorter events, 0.0 us)
Async XLA Ops:
  0.0 12.4 %copy-start.2 = (bf16[1,16,68,512]{3,1,2,0:T(8,128)(2,1)S(1)}, bf16[1,16,68,512]{3,1,2,0:T(8,128)(2,1)}, u32[]{:S(2)}) copy-start(bf16[1,16,68,512]{3,1,2,0:T(8,128)(2,1)} %param.9) | copy-start | bytes 3342340
  1.3 14.0 %collective-permute-start.4 = (bf16[128,1792]{1,0:T(8,128)(2,1)S(1)}, bf16[128,1792]{1,0:T(8,128)(2,1)S(1)}, u32[]{:S(2)}, u32[]{:S(2)}) collective-permute-start(bf16[128,1792]{1,0:T(8,128)(2,1)S(1)} %bitcast_select_fusion), channel_id=1, source_target_pairs={{0,26},{1,27},{2,28},{3,29},{4,30},{5,31},{6,24},{7,25},{8,2},{9,3... | collective-permute-start | bytes 1376264 | tf_op jit(solution)/shard_map/ppermute | solution.py:230
  4.6 13.6 %collective-permute-start = (bf16[128,1792]{1,0:T(8,128)(2,1)S(1)}, bf16[128,1792]{1,0:T(8,128)(2,1)S(1)}, u32[]{:S(2)}, u32[]{:S(2)}) collective-permute-start(bf16[128,1792]{1,0:T(8,128)(2,1)S(1)} %bitcast_select_fusion), channel_id=1, source_target_pairs={{0,25},{1,24},{2,27},{3,26},{4,29},{5,28},{6,31},{7,30},{8,1},{9,0... | collective-permute-start | bytes 1376264 | tf_op jit(solution)/shard_map/ppermute | solution.py:230
  6.4 0.7 %copy-start = (s32[1,128,8]{1,2,0:T(8,128)S(1)}, s32[1,128,8]{1,2,0:T(8,128)}, u32[]{:S(2)}) copy-start(s32[1,128,8]{1,2,0:T(8,128)} %param.8) | copy-start | bytes 12292
  7.1 0.7 %copy-start.1 = (bf16[1,128,8]{1,2,0:T(8,128)(2,1)S(1)}, bf16[1,128,8]{1,2,0:T(8,128)(2,1)}, u32[]{:S(2)}) copy-start(bf16[1,128,8]{1,2,0:T(8,128)(2,1)} %param.7) | copy-start | bytes 6148
  7.8 8.7 %collective-permute-start.3 = (bf16[16,128]{1,0:T(8,128)(2,1)S(1)}, bf16[16,128]{1,0:T(8,128)(2,1)S(1)}, u32[]{:S(2)}, u32[]{:S(2)}) collective-permute-start(bf16[16,128]{1,0:T(8,128)(2,1)S(1)} %notes.1.refs_0_), channel_id=1, source_target_pairs={{0,6},{1,7},{2,0},{3,1},{4,2},{5,3},{6,4},{7,5},{8,14},{9,15},{10,... | collective-permute-start | bytes 12296 | tf_op jit(solution)/shard_map/ppermute | solution.py:230
  10.0 8.2 %collective-permute-start.2 = (bf16[16,128]{1,0:T(8,128)(2,1)S(1)}, bf16[16,128]{1,0:T(8,128)(2,1)S(1)}, u32[]{:S(2)}, u32[]{:S(2)}) collective-permute-start(bf16[16,128]{1,0:T(8,128)(2,1)S(1)} %notes.1.refs_0_), channel_id=1, source_target_pairs={{0,4},{1,5},{2,6},{3,7},{4,0},{5,1},{6,2},{7,3},{8,12},{9,13},{10,... | collective-permute-start | bytes 12296 | tf_op jit(solution)/shard_map/ppermute | solution.py:230
  10.8 7.4 %collective-permute-start.1 = (bf16[16,128]{1,0:T(8,128)(2,1)S(1)}, bf16[16,128]{1,0:T(8,128)(2,1)S(1)}, u32[]{:S(2)}, u32[]{:S(2)}) collective-permute-start(bf16[16,128]{1,0:T(8,128)(2,1)S(1)} %notes.1.refs_0_), channel_id=1, source_target_pairs={{0,2},{1,3},{2,4},{3,5},{4,6},{5,7},{6,0},{7,1},{8,10},{9,11},{10,... | collective-permute-start | bytes 12296 | tf_op jit(solution)/shard_map/ppermute | solution.py:230
  15.3 13.3 %collective-permute-start.5 = (bf16[128,1792]{1,0:T(8,128)(2,1)S(1)}, bf16[128,1792]{1,0:T(8,128)(2,1)S(1)}, u32[]{:S(2)}, u32[]{:S(2)}) collective-permute-start(bf16[128,1792]{1,0:T(8,128)(2,1)S(1)} %collective-permute-done.4.refs_0_), channel_id=1, source_target_pairs={{0,2},{1,3},{2,4},{3,5},{4,6},{5,7},{6,0},{7,1},{8,10},{9,11},{10,... | collective-permute-start | bytes 1376264 | tf_op jit(solution)/shard_map/ppermute | solution.py:230
  16.5 13.0 %collective-permute-start.6 = (bf16[128,1792]{1,0:T(8,128)(2,1)S(1)}, bf16[128,1792]{1,0:T(8,128)(2,1)S(1)}, u32[]{:S(2)}, u32[]{:S(2)}) collective-permute-start(bf16[128,1792]{1,0:T(8,128)(2,1)S(1)} %collective-permute-done.4.refs_0_), channel_id=1, source_target_pairs={{0,1},{1,0},{2,3},{3,2},{4,5},{5,4},{6,7},{7,6},{8,9},{9,8},{10,11... | collective-permute-start | bytes 1376264 | tf_op jit(solution)/shard_map/ppermute | solution.py:230
  18.2 22.0 %collective-permute-start.8 = (bf16[128,1792]{1,0:T(8,128)(2,1)S(1)}, bf16[128,1792]{1,0:T(8,128)(2,1)S(1)}, u32[]{:S(2)}, u32[]{:S(2)}) collective-permute-start(bf16[128,1792]{1,0:T(8,128)(2,1)S(1)} %bitcast_select_fusion), channel_id=1, source_target_pairs={{0,30},{1,31},{2,24},{3,25},{4,26},{5,27},{6,28},{7,29},{8,6},{9,7... | collective-permute-start | bytes 1376264 | tf_op jit(solution)/shard_map/ppermute | solution.py:230
  23.5 17.0 %collective-permute-start.10 = (bf16[128,1792]{1,0:T(8,128)(2,1)S(1)}, bf16[128,1792]{1,0:T(8,128)(2,1)S(1)}, u32[]{:S(2)}, u32[]{:S(2)}) collective-permute-start(bf16[128,1792]{1,0:T(8,128)(2,1)S(1)} %bitcast_select_fusion), channel_id=1, source_target_pairs={{0,24},{1,25},{2,26},{3,27},{4,28},{5,29},{6,30},{7,31},{8,0},{9,1... | collective-permute-start | bytes 1376264 | tf_op jit(solution)/shard_map/ppermute | solution.py:230
  29.5 25.1 %collective-permute-start.7 = (bf16[128,1792]{1,0:T(8,128)(2,1)S(1)}, bf16[128,1792]{1,0:T(8,128)(2,1)S(1)}, u32[]{:S(2)}, u32[]{:S(2)}) collective-permute-start(bf16[128,1792]{1,0:T(8,128)(2,1)S(1)} %collective-permute-done.5.refs_1_), channel_id=1, source_target_pairs={{0,1},{1,0},{2,3},{3,2},{4,5},{5,4},{6,7},{7,6},{8,9},{9,8},{10,11... | collective-permute-start | bytes 1376264 | tf_op jit(solution)/shard_map/ppermute | solution.py:230
  40.2 14.4 %collective-permute-start.9 = (bf16[128,1792]{1,0:T(8,128)(2,1)S(1)}, bf16[128,1792]{1,0:T(8,128)(2,1)S(1)}, u32[]{:S(2)}, u32[]{:S(2)}) collective-permute-start(bf16[128,1792]{1,0:T(8,128)(2,1)S(1)} %collective-permute-done.8.refs_3_), channel_id=1, source_target_pairs={{0,1},{1,0},{2,3},{3,2},{4,5},{5,4},{6,7},{7,6},{8,9},{9,8},{10,11... | collective-permute-start | bytes 1376264 | tf_op jit(solution)/shard_map/ppermute | solution.py:230
where the time goes:
time: 67.9 us; the launch traced here: 67.4 us
  Pallas kernels  27.4 us (40%)
  starting transfers between devices  22.7 us (33%)
  waiting for transfers between devices  14 us (21%)
  local copies, waits for them, and re-layouts  1.99 us (3%)
  other arithmetic  1.3 us (2%)
    pallas_call x2, Pallas kernels, grad_into(): pl.pallas_call(functools.partial(grad_kernel, n_expert, other, early), ou...  25 us
    ppermute x11, starting transfers between devices, turned(): return lax.ppermute(array, axes, pairs)  22.7 us
    ppermute x11, waiting for transfers between devices, turned(): return lax.ppermute(array, axes, pairs)  14 us
    pallas_call x4, Pallas kernels, small_call(): pl.pallas_call(kernel, out_shape=[jax.ShapeDtypeStruct(shape, jnp.bfloat1...  2.39 us
    unnamed x7, local copies, waits for them, and re-layouts  1.99 us
  transfers between devices with their start and end apart: 11, of which 4 were waited for; matrix products, arithmetic and copies ran while one was open for 1% of the time, Pallas kernels for 22%

commit v1 on v0

--- a/solution.py
+++ b/solution.py
@@ -293,13 +293,17 @@
     last = n_expert - 1
     early = tuple(range(1, last))
     own = weighed(blocks, early)
+    others = {t: weighed({0: beside[0][t]}, (0,)) for t in range(1, n_tensor)}
     for k in range(1, n_expert):
         if k == last - 1:
-            blocks[k], own, beside[k - 1] = lax.optimization_barrier((blocks[k], own, beside[k - 1]))
+            blocks[k], own, others, beside[k - 1] = lax.optimization_barrier(
+                (blocks[k], own, others, beside[k - 1])
+            )
         beside[k] = {t: turned(blocks[k], 0, 0, t) for t in range(1, n_tensor)}
     out = grad_into(None, [own.get(k, blocks[k]) for k in range(n_expert)], 0, early)
     for t in range(1, n_tensor):
-        out = grad_into(out, [beside[k][t] for k in range(n_expert)], n_tensor - t, ())
+        sources = [others[t].get(k, beside[k][t]) for k in range(n_expert)]
+        out = grad_into(out, sources, n_tensor - t, (0,))
     return out[None]
 
 

time: 67.9 us -> 67.6 us (level)
    pallas_call x4 -> x5, Pallas kernels: 2.39 us -> 2.98 us  [small_call(): pl.pallas_call(kernel, out_shape=[jax.ShapeDtypeStruct(shape, jnp.bfloat1...]
  transfers between devices with their start and end apart: 11 -> 11, of which waited for: 4 -> 4; matrix products, arithmetic and copies ran while one was open for 1% -> 1% of each run, Pallas kernels for 22% -> 23%
where the time goes in v1:
time: 67.6 us; the launch traced here: 67.1 us
  Pallas kernels  27.7 us (41%)
  starting transfers between devices  22.7 us (34%)
  waiting for transfers between devices  13.4 us (20%)
  local copies, waits for them, and re-layouts  1.99 us (3%)
  other arithmetic  1.3 us (2%)
    pallas_call x2, Pallas kernels, grad_into(): pl.pallas_call(functools.partial(grad_kernel, n_expert, other, early), ou...  24.7 us
    ppermute x11, starting transfers between devices, turned(): return lax.ppermute(array, axes, pairs)  22.7 us
    ppermute x11, waiting for transfers between devices, turned(): return lax.ppermute(array, axes, pairs)  13.4 us
    pallas_call x5, Pallas kernels, small_call(): pl.pallas_call(kernel, out_shape=[jax.ShapeDtypeStruct(shape, jnp.bfloat1...  2.98 us
    unnamed x7, local copies, waits for them, and re-layouts  1.99 us
  transfers between devices with their start and end apart: 11, of which 4 were waited for; matrix products, arithmetic and copies ran while one was open for 1% of the time, Pallas kernels for 23%

profile of v1, /device:TPU:0, one launch (start us, length us, event | category | flops | bytes accessed | tf_op | source)
XLA Modules:
  0.0 67.1 jit_solution(1116891890161892010)
XLA Ops:
  0.0 0.0 copy-start.2
  0.0 1.3 %bitcast_select_fusion = bf16[128,1792]{1,0:T(8,128)(2,1)S(1)} fusion(bf16[128,1792]{1,0:T(8,128)(2,1)} %param.6, bf16[1,128,1792]{2,1,0:T(8,128)(2,1)} %param.5, pred[]{:T(512)S(6)} %eq.3), kind=kLoop, calls=%fused_computation.1 | loop fusion | flops 229376 | bytes 1376257 | tf_op jit(solution)/shard_map/jit(_where)/select_n | solution.py:260
  1.3 3.3 %collective-permute-start.4 = (bf16[128,1792]{1,0:T(8,128)(2,1)S(1)}, bf16[128,1792]{1,0:T(8,128)(2,1)S(1)}, u32[]{:S(2)}, u32[]{:S(2)}) collective-permute-start(bf16[128,1792]{1,0:T(8,128)(2,1)S(1)} %bitcast_select_fusion), channel_id=1, source_target_pairs={{0,26},{1,27},{2,28},{3,29},{4,30},{5,31},{6,24},{7,25},{8,2},{9,3... | collective-permute-start | bytes 1376264 | tf_op jit(solution)/shard_map/ppermute | solution.py:230
  4.6 1.8 %collective-permute-start = (bf16[128,1792]{1,0:T(8,128)(2,1)S(1)}, bf16[128,1792]{1,0:T(8,128)(2,1)S(1)}, u32[]{:S(2)}, u32[]{:S(2)}) collective-permute-start(bf16[128,1792]{1,0:T(8,128)(2,1)S(1)} %bitcast_select_fusion), channel_id=1, source_target_pairs={{0,25},{1,24},{2,27},{3,26},{4,29},{5,28},{6,31},{7,30},{8,1},{9,0... | collective-permute-start | bytes 1376264 | tf_op jit(solution)/shard_map/ppermute | solution.py:230
  6.4 0.0 copy-start
  6.4 0.7 %copy-done = s32[1,128,8]{1,2,0:T(8,128)S(1)} copy-done((s32[1,128,8]{1,2,0:T(8,128)S(1)}, s32[1,128,8]{1,2,0:T(8,128)}, u32[]{:S(2)}) %copy-start) | copy-done | bytes 4120
  7.1 0.0 copy-start.1
  7.1 0.7 %copy-done.1 = bf16[1,128,8]{1,2,0:T(8,128)(2,1)S(1)} copy-done((bf16[1,128,8]{1,2,0:T(8,128)(2,1)S(1)}, bf16[1,128,8]{1,2,0:T(8,128)(2,1)}, u32[]{:S(2)}) %copy-start.1) | copy-done | bytes 2072
  7.8 2.2 %collective-permute-start.3 = (bf16[16,128]{1,0:T(8,128)(2,1)S(1)}, bf16[16,128]{1,0:T(8,128)(2,1)S(1)}, u32[]{:S(2)}, u32[]{:S(2)}) collective-permute-start(bf16[16,128]{1,0:T(8,128)(2,1)S(1)} %notes.1.refs_0_), channel_id=1, source_target_pairs={{0,6},{1,7},{2,0},{3,1},{4,2},{5,3},{6,4},{7,5},{8,14},{9,15},{10,... | collective-permute-start | bytes 12296 | tf_op jit(solution)/shard_map/ppermute | solution.py:230
  10.0 0.8 %collective-permute-start.2 = (bf16[16,128]{1,0:T(8,128)(2,1)S(1)}, bf16[16,128]{1,0:T(8,128)(2,1)S(1)}, u32[]{:S(2)}, u32[]{:S(2)}) collective-permute-start(bf16[16,128]{1,0:T(8,128)(2,1)S(1)} %notes.1.refs_0_), channel_id=1, source_target_pairs={{0,4},{1,5},{2,6},{3,7},{4,0},{5,1},{6,2},{7,3},{8,12},{9,13},{10,... | collective-permute-start | bytes 12296 | tf_op jit(solution)/shard_map/ppermute | solution.py:230
  10.8 1.6 %collective-permute-start.1 = (bf16[16,128]{1,0:T(8,128)(2,1)S(1)}, bf16[16,128]{1,0:T(8,128)(2,1)S(1)}, u32[]{:S(2)}, u32[]{:S(2)}) collective-permute-start(bf16[16,128]{1,0:T(8,128)(2,1)S(1)} %notes.1.refs_0_), channel_id=1, source_target_pairs={{0,2},{1,3},{2,4},{3,5},{4,6},{5,7},{6,0},{7,1},{8,10},{9,11},{10,... | collective-permute-start | bytes 12296 | tf_op jit(solution)/shard_map/ppermute | solution.py:230
  12.4 0.0 copy-done.2
  12.4 0.6 copy.9
  13.0 0.8 %turn.1.act_ref = bf16[16,512,128]{2,1,0:T(8,128)(2,1)S(1)} custom-call(bf16[16,68,512]{2,1,0:T(8,128)(2,1)S(1)} %bitcast.12), custom_call_target="tpu_custom_call" | custom-call | tf_op jit(solution)/shard_map/turn/pallas_call | solution.py:209
  13.8 1.6 %collective-permute-done.4.refs_0_ = bf16[128,1792]{1,0:T(8,128)(2,1)S(1)} collective-permute-done((bf16[128,1792]{1,0:T(8,128)(2,1)S(1)}, bf16[128,1792]{1,0:T(8,128)(2,1)S(1)}, u32[]{:S(2)}, u32[]{:S(2)}) %collective-permute-start.4) | collective-permute-done | bytes 458784 | tf_op jit(solution)/shard_map/ppermute | solution.py:230
  15.3 1.2 %collective-permute-start.5 = (bf16[128,1792]{1,0:T(8,128)(2,1)S(1)}, bf16[128,1792]{1,0:T(8,128)(2,1)S(1)}, u32[]{:S(2)}, u32[]{:S(2)}) collective-permute-start(bf16[128,1792]{1,0:T(8,128)(2,1)S(1)} %collective-permute-done.4.refs_0_), channel_id=1, source_target_pairs={{0,2},{1,3},{2,4},{3,5},{4,6},{5,7},{6,0},{7,1},{8,10},{9,11},{10,... | collective-permute-start | bytes 1376264 | tf_op jit(solution)/shard_map/ppermute | solution.py:230
  16.5 0.0 collective-permute-done.3.refs_3_
  16.5 1.7 %collective-permute-start.6 = (bf16[128,1792]{1,0:T(8,128)(2,1)S(1)}, bf16[128,1792]{1,0:T(8,128)(2,1)S(1)}, u32[]{:S(2)}, u32[]{:S(2)}) collective-permute-start(bf16[128,1792]{1,0:T(8,128)(2,1)S(1)} %collective-permute-done.4.refs_0_), channel_id=1, source_target_pairs={{0,1},{1,0},{2,3},{3,2},{4,5},{5,4},{6,7},{7,6},{8,9},{9,8},{10,11... | collective-permute-start | bytes 1376264 | tf_op jit(solution)/shard_map/ppermute | solution.py:230
  18.2 0.0 collective-permute-done.2.refs_2_
  18.2 0.0 collective-permute-done.1.refs_1_
  18.2 0.0 collective-permute-done.refs_0_
  18.2 5.2 %collective-permute-start.8 = (bf16[128,1792]{1,0:T(8,128)(2,1)S(1)}, bf16[128,1792]{1,0:T(8,128)(2,1)S(1)}, u32[]{:S(2)}, u32[]{:S(2)}) collective-permute-start(bf16[128,1792]{1,0:T(8,128)(2,1)S(1)} %bitcast_select_fusion), channel_id=1, source_target_pairs={{0,30},{1,31},{2,24},{3,25},{4,26},{5,27},{6,28},{7,29},{8,6},{9,7... | collective-permute-start | bytes 1376264 | tf_op jit(solution)/shard_map/ppermute | solution.py:230
  23.5 0.3 collective-permute-start.10
  23.7 0.7 %place.1.place_ref = bf16[4,272,128]{2,1,0:T(8,128)(2,1)S(1)} custom-call(bf16[16,128]{1,0:T(8,128)(2,1)S(1)} %notes.1.refs_0_, bf16[16,128]{1,0:T(8,128)(2,1)S(1)} %collective-permute-done.1.refs_1_, bf16[16,128]{1,0:T(8,128)(2,1)S(1)} %collective-permute-done.2.refs_2_, bf16[16,128]{1,0:T(8,128)(2,1)S(1)} %collective-permute-done.3.refs_3_), custom_call_target="tpu_custom_call" | custom-call | tf_op jit(solution)/shard_map/place/pallas_call | solution.py:209
  24.5 0.6 early.3.refs_0_
  25.1 3.5 %collective-permute-done.5.refs_1_ = bf16[128,1792]{1,0:T(8,128)(2,1)S(1)} collective-permute-done((bf16[128,1792]{1,0:T(8,128)(2,1)S(1)}, bf16[128,1792]{1,0:T(8,128)(2,1)S(1)}, u32[]{:S(2)}, u32[]{:S(2)}) %collective-permute-start.5) | collective-permute-done | bytes 458784 | tf_op jit(solution)/shard_map/ppermute | solution.py:230
  28.6 0.9 %early.2 = (bf16[272,1792]{1,0:T(8,128)(2,1)S(1)}, bf16[272,1792]{1,0:T(8,128)(2,1)S(1)}) custom-call(bf16[4,272,128]{2,1,0:T(8,128)(2,1)S(1)} %place.1.place_ref, bf16[128,1792]{1,0:T(8,128)(2,1)S(1)} %collective-permute-done.4.refs_0_, bf16[128,1792]{1,0:T(8,128)(2,1)S(1)} %collective-permute-done.5.refs_1_), custom_call_target="tpu_custom_call" | custom-call | tf_op jit(solution)/shard_map/early/pallas_call | solution.py:209
  29.5 0.0 collective-permute-done.6.refs_1_
  29.5 4.4 %collective-permute-start.7 = (bf16[128,1792]{1,0:T(8,128)(2,1)S(1)}, bf16[128,1792]{1,0:T(8,128)(2,1)S(1)}, u32[]{:S(2)}, u32[]{:S(2)}) collective-permute-start(bf16[128,1792]{1,0:T(8,128)(2,1)S(1)} %collective-permute-done.5.refs_1_), channel_id=1, source_target_pairs={{0,1},{1,0},{2,3},{3,2},{4,5},{5,4},{6,7},{7,6},{8,9},{9,8},{10,11... | collective-permute-start | bytes 1376264 | tf_op jit(solution)/shard_map/ppermute | solution.py:230
  33.9 6.3 %collective-permute-done.8.refs_3_ = bf16[128,1792]{1,0:T(8,128)(2,1)S(1)} collective-permute-done((bf16[128,1792]{1,0:T(8,128)(2,1)S(1)}, bf16[128,1792]{1,0:T(8,128)(2,1)S(1)}, u32[]{:S(2)}, u32[]{:S(2)}) %collective-permute-start.8) | collective-permute-done | bytes 458784 | tf_op jit(solution)/shard_map/ppermute | solution.py:230
  40.2 0.2 collective-permute-start.9
  40.4 0.0 collective-permute-done.10.refs_0_
  40.4 12.2 %weight_grad.2.refs_4_ = bf16[16,512,3584]{2,1,0:T(8,128)(2,1)} custom-call(bf16[4,272,128]{2,1,0:T(8,128)(2,1)S(1)} %place.1.place_ref, bf16[16,512,128]{2,1,0:T(8,128)(2,1)S(1)} %turn.1.act_ref, bf16[128,1792]{1,0:T(8,128)(2,1)S(1)} %collective-permute-done.10.refs_0_, bf16[272,1792]{1,0:T(8,128)(2,1)S(1)} %get-tuple-element.29.refs_1_, ...), custom_call_target="tpu_custom_call" | custom-call | flops 7516192768 | bytes 29360128 | tf_op jit(solution)/shard_map/weight_grad/pallas_call | solution.py:240
  52.7 1.9 %collective-permute-done.9.refs_3_ = bf16[128,1792]{1,0:T(8,128)(2,1)S(1)} collective-permute-done((bf16[128,1792]{1,0:T(8,128)(2,1)S(1)}, bf16[128,1792]{1,0:T(8,128)(2,1)S(1)}, u32[]{:S(2)}, u32[]{:S(2)}) %collective-permute-start.9) | collective-permute-done | bytes 458784 | tf_op jit(solution)/shard_map/ppermute | solution.py:230
  54.6 0.0 collective-permute-done.7.refs_2_
  54.6 12.5 %weight_grad.3 = bf16[16,512,3584]{2,1,0:T(8,128)(2,1)} custom-call(bf16[4,272,128]{2,1,0:T(8,128)(2,1)S(1)} %place.1.place_ref, bf16[16,512,128]{2,1,0:T(8,128)(2,1)S(1)} %turn.1.act_ref, bf16[272,1792]{1,0:T(8,128)(2,1)S(1)} %early.3.refs_0_, bf16[128,1792]{1,0:T(8,128)(2,1)S(1)} %collective-permute-done.6.refs_1_, ...), custom_call_target="tpu_custom_call", output_to_operand_aliasing={{}: (6, {})} | custom-call | flops 7516192768 | bytes 29360128 | tf_op jit(solution)/shard_map/weight_grad/pallas_call | solution.py:240
  (1 shorter events, 0.0 us)
Async XLA Ops:
  0.0 12.4 %copy-start.2 = (bf16[1,16,68,512]{3,1,2,0:T(8,128)(2,1)S(1)}, bf16[1,16,68,512]{3,1,2,0:T(8,128)(2,1)}, u32[]{:S(2)}) copy-start(bf16[1,16,68,512]{3,1,2,0:T(8,128)(2,1)} %param.9) | copy-start | bytes 3342340
  1.3 14.0 %collective-permute-start.4 = (bf16[128,1792]{1,0:T(8,128)(2,1)S(1)}, bf16[128,1792]{1,0:T(8,128)(2,1)S(1)}, u32[]{:S(2)}, u32[]{:S(2)}) collective-permute-start(bf16[128,1792]{1,0:T(8,128)(2,1)S(1)} %bitcast_select_fusion), channel_id=1, source_target_pairs={{0,26},{1,27},{2,28},{3,29},{4,30},{5,31},{6,24},{7,25},{8,2},{9,3... | collective-permute-start | bytes 1376264 | tf_op jit(solution)/shard_map/ppermute | solution.py:230
  4.6 13.6 %collective-permute-start = (bf16[128,1792]{1,0:T(8,128)(2,1)S(1)}, bf16[128,1792]{1,0:T(8,128)(2,1)S(1)}, u32[]{:S(2)}, u32[]{:S(2)}) collective-permute-start(bf16[128,1792]{1,0:T(8,128)(2,1)S(1)} %bitcast_select_fusion), channel_id=1, source_target_pairs={{0,25},{1,24},{2,27},{3,26},{4,29},{5,28},{6,31},{7,30},{8,1},{9,0... | collective-permute-start | bytes 1376264 | tf_op jit(solution)/shard_map/ppermute | solution.py:230
  6.4 0.7 %copy-start = (s32[1,128,8]{1,2,0:T(8,128)S(1)}, s32[1,128,8]{1,2,0:T(8,128)}, u32[]{:S(2)}) copy-start(s32[1,128,8]{1,2,0:T(8,128)} %param.8) | copy-start | bytes 12292
  7.1 0.7 %copy-start.1 = (bf16[1,128,8]{1,2,0:T(8,128)(2,1)S(1)}, bf16[1,128,8]{1,2,0:T(8,128)(2,1)}, u32[]{:S(2)}) copy-start(bf16[1,128,8]{1,2,0:T(8,128)(2,1)} %param.7) | copy-start | bytes 6148
  7.8 8.7 %collective-permute-start.3 = (bf16[16,128]{1,0:T(8,128)(2,1)S(1)}, bf16[16,128]{1,0:T(8,128)(2,1)S(1)}, u32[]{:S(2)}, u32[]{:S(2)}) collective-permute-start(bf16[16,128]{1,0:T(8,128)(2,1)S(1)} %notes.1.refs_0_), channel_id=1, source_target_pairs={{0,6},{1,7},{2,0},{3,1},{4,2},{5,3},{6,4},{7,5},{8,14},{9,15},{10,... | collective-permute-start | bytes 12296 | tf_op jit(solution)/shard_map/ppermute | solution.py:230
  10.0 8.2 %collective-permute-start.2 = (bf16[16,128]{1,0:T(8,128)(2,1)S(1)}, bf16[16,128]{1,0:T(8,128)(2,1)S(1)}, u32[]{:S(2)}, u32[]{:S(2)}) collective-permute-start(bf16[16,128]{1,0:T(8,128)(2,1)S(1)} %notes.1.refs_0_), channel_id=1, source_target_pairs={{0,4},{1,5},{2,6},{3,7},{4,0},{5,1},{6,2},{7,3},{8,12},{9,13},{10,... | collective-permute-start | bytes 12296 | tf_op jit(solution)/shard_map/ppermute | solution.py:230
  10.8 7.4 %collective-permute-start.1 = (bf16[16,128]{1,0:T(8,128)(2,1)S(1)}, bf16[16,128]{1,0:T(8,128)(2,1)S(1)}, u32[]{:S(2)}, u32[]{:S(2)}) collective-permute-start(bf16[16,128]{1,0:T(8,128)(2,1)S(1)} %notes.1.refs_0_), channel_id=1, source_target_pairs={{0,2},{1,3},{2,4},{3,5},{4,6},{5,7},{6,0},{7,1},{8,10},{9,11},{10,... | collective-permute-start | bytes 12296 | tf_op jit(solution)/shard_map/ppermute | solution.py:230
  15.3 13.3 %collective-permute-start.5 = (bf16[128,1792]{1,0:T(8,128)(2,1)S(1)}, bf16[128,1792]{1,0:T(8,128)(2,1)S(1)}, u32[]{:S(2)}, u32[]{:S(2)}) collective-permute-start(bf16[128,1792]{1,0:T(8,128)(2,1)S(1)} %collective-permute-done.4.refs_0_), channel_id=1, source_target_pairs={{0,2},{1,3},{2,4},{3,5},{4,6},{5,7},{6,0},{7,1},{8,10},{9,11},{10,... | collective-permute-start | bytes 1376264 | tf_op jit(solution)/shard_map/ppermute | solution.py:230
  16.5 13.0 %collective-permute-start.6 = (bf16[128,1792]{1,0:T(8,128)(2,1)S(1)}, bf16[128,1792]{1,0:T(8,128)(2,1)S(1)}, u32[]{:S(2)}, u32[]{:S(2)}) collective-permute-start(bf16[128,1792]{1,0:T(8,128)(2,1)S(1)} %collective-permute-done.4.refs_0_), channel_id=1, source_target_pairs={{0,1},{1,0},{2,3},{3,2},{4,5},{5,4},{6,7},{7,6},{8,9},{9,8},{10,11... | collective-permute-start | bytes 1376264 | tf_op jit(solution)/shard_map/ppermute | solution.py:230
  18.2 22.0 %collective-permute-start.8 = (bf16[128,1792]{1,0:T(8,128)(2,1)S(1)}, bf16[128,1792]{1,0:T(8,128)(2,1)S(1)}, u32[]{:S(2)}, u32[]{:S(2)}) collective-permute-start(bf16[128,1792]{1,0:T(8,128)(2,1)S(1)} %bitcast_select_fusion), channel_id=1, source_target_pairs={{0,30},{1,31},{2,24},{3,25},{4,26},{5,27},{6,28},{7,29},{8,6},{9,7... | collective-permute-start | bytes 1376264 | tf_op jit(solution)/shard_map/ppermute | solution.py:230
  23.5 17.0 %collective-permute-start.10 = (bf16[128,1792]{1,0:T(8,128)(2,1)S(1)}, bf16[128,1792]{1,0:T(8,128)(2,1)S(1)}, u32[]{:S(2)}, u32[]{:S(2)}) collective-permute-start(bf16[128,1792]{1,0:T(8,128)(2,1)S(1)} %bitcast_select_fusion), channel_id=1, source_target_pairs={{0,24},{1,25},{2,26},{3,27},{4,28},{5,29},{6,30},{7,31},{8,0},{9,1... | collective-permute-start | bytes 1376264 | tf_op jit(solution)/shard_map/ppermute | solution.py:230
  29.5 25.1 %collective-permute-start.7 = (bf16[128,1792]{1,0:T(8,128)(2,1)S(1)}, bf16[128,1792]{1,0:T(8,128)(2,1)S(1)}, u32[]{:S(2)}, u32[]{:S(2)}) collective-permute-start(bf16[128,1792]{1,0:T(8,128)(2,1)S(1)} %collective-permute-done.5.refs_1_), channel_id=1, source_target_pairs={{0,1},{1,0},{2,3},{3,2},{4,5},{5,4},{6,7},{7,6},{8,9},{9,8},{10,11... | collective-permute-start | bytes 1376264 | tf_op jit(solution)/shard_map/ppermute | solution.py:230
  40.2 14.4 %collective-permute-start.9 = (bf16[128,1792]{1,0:T(8,128)(2,1)S(1)}, bf16[128,1792]{1,0:T(8,128)(2,1)S(1)}, u32[]{:S(2)}, u32[]{:S(2)}) collective-permute-start(bf16[128,1792]{1,0:T(8,128)(2,1)S(1)} %collective-permute-done.8.refs_3_), channel_id=1, source_target_pairs={{0,1},{1,0},{2,3},{3,2},{4,5},{5,4},{6,7},{7,6},{8,9},{9,8},{10,11... | collective-permute-start | bytes 1376264 | tf_op jit(solution)/shard_map/ppermute | solution.py:230

commit v2 on v1

--- a/solution.py
+++ b/solution.py
@@ -296,9 +296,9 @@
     others = {t: weighed({0: beside[0][t]}, (0,)) for t in range(1, n_tensor)}
     for k in range(1, n_expert):
         if k == last - 1:
-            blocks[k], own, others, beside[k - 1] = lax.optimization_barrier(
-                (blocks[k], own, others, beside[k - 1])
-            )
+            blocks[k], others = lax.optimization_barrier((blocks[k], others))
+        if k == last:
+            blocks[k], own, beside[1] = lax.optimization_barrier((blocks[k], own, beside[1]))
         beside[k] = {t: turned(blocks[k], 0, 0, t) for t in range(1, n_tensor)}
     out = grad_into(None, [own.get(k, blocks[k]) for k in range(n_expert)], 0, early)
     for t in range(1, n_tensor):

time: 67.6 us -> 67.3 us (level)
  starting transfers between devices: 22.7 us -> 22 us
  transfers between devices with their start and end apart: 11 -> 11, of which waited for: 4 -> 5; matrix products, arithmetic and copies ran while one was open for 1% -> 1% of each run, Pallas kernels for 23% -> 23%
where the time goes in v2:
time: 67.3 us; the launch traced here: 66.1 us
  Pallas kernels  27.7 us (41%)
  starting transfers between devices  22 us (33%)
  waiting for transfers between devices  13.1 us (19%)
  local copies, waits for them, and re-layouts  1.99 us (3%)
  other arithmetic  1.3 us (2%)
    pallas_call x2, Pallas kernels, grad_into(): pl.pallas_call(functools.partial(grad_kernel, n_expert, other, early), ou...  24.7 us
    ppermute x11, starting transfers between devices, turned(): return lax.ppermute(array, axes, pairs)  22 us
    ppermute x11, waiting for transfers between devices, turned(): return lax.ppermute(array, axes, pairs)  13.1 us
    pallas_call x5, Pallas kernels, small_call(): pl.pallas_call(kernel, out_shape=[jax.ShapeDtypeStruct(shape, jnp.bfloat1...  2.97 us
    unnamed x7, local copies, waits for them, and re-layouts  1.99 us
  transfers between devices with their start and end apart: 11, of which 5 were waited for; matrix products, arithmetic and copies ran while one was open for 1% of the time, Pallas kernels for 23%

profile of v2, /device:TPU:0, one launch (start us, length us, event | category | flops | bytes accessed | tf_op | source)
XLA Modules:
  0.0 66.1 jit_solution(16241958159638656680)
XLA Ops:
  0.0 0.0 copy-start.2
  0.0 1.3 %bitcast_select_fusion = bf16[128,1792]{1,0:T(8,128)(2,1)S(1)} fusion(bf16[128,1792]{1,0:T(8,128)(2,1)} %param.6, bf16[1,128,1792]{2,1,0:T(8,128)(2,1)} %param.5, pred[]{:T(512)S(6)} %eq.3), kind=kLoop, calls=%fused_computation.1 | loop fusion | flops 229376 | bytes 1376257 | tf_op jit(solution)/shard_map/jit(_where)/select_n | solution.py:260
  1.3 3.3 %collective-permute-start.4 = (bf16[128,1792]{1,0:T(8,128)(2,1)S(1)}, bf16[128,1792]{1,0:T(8,128)(2,1)S(1)}, u32[]{:S(2)}, u32[]{:S(2)}) collective-permute-start(bf16[128,1792]{1,0:T(8,128)(2,1)S(1)} %bitcast_select_fusion), channel_id=1, source_target_pairs={{0,26},{1,27},{2,28},{3,29},{4,30},{5,31},{6,24},{7,25},{8,2},{9,3... | collective-permute-start | bytes 1376264 | tf_op jit(solution)/shard_map/ppermute | solution.py:230
  4.6 1.8 %collective-permute-start = (bf16[128,1792]{1,0:T(8,128)(2,1)S(1)}, bf16[128,1792]{1,0:T(8,128)(2,1)S(1)}, u32[]{:S(2)}, u32[]{:S(2)}) collective-permute-start(bf16[128,1792]{1,0:T(8,128)(2,1)S(1)} %bitcast_select_fusion), channel_id=1, source_target_pairs={{0,25},{1,24},{2,27},{3,26},{4,29},{5,28},{6,31},{7,30},{8,1},{9,0... | collective-permute-start | bytes 1376264 | tf_op jit(solution)/shard_map/ppermute | solution.py:230
  6.4 0.0 copy-start
  6.4 0.7 %copy-done = s32[1,128,8]{1,2,0:T(8,128)S(1)} copy-done((s32[1,128,8]{1,2,0:T(8,128)S(1)}, s32[1,128,8]{1,2,0:T(8,128)}, u32[]{:S(2)}) %copy-start) | copy-done | bytes 4120
  7.1 0.0 copy-start.1
  7.1 0.7 %copy-done.1 = bf16[1,128,8]{1,2,0:T(8,128)(2,1)S(1)} copy-done((bf16[1,128,8]{1,2,0:T(8,128)(2,1)S(1)}, bf16[1,128,8]{1,2,0:T(8,128)(2,1)}, u32[]{:S(2)}) %copy-start.1) | copy-done | bytes 2072
  7.8 2.2 %collective-permute-start.3 = (bf16[16,128]{1,0:T(8,128)(2,1)S(1)}, bf16[16,128]{1,0:T(8,128)(2,1)S(1)}, u32[]{:S(2)}, u32[]{:S(2)}) collective-permute-start(bf16[16,128]{1,0:T(8,128)(2,1)S(1)} %notes.1.refs_0_), channel_id=1, source_target_pairs={{0,6},{1,7},{2,0},{3,1},{4,2},{5,3},{6,4},{7,5},{8,14},{9,15},{10,... | collective-permute-start | bytes 12296 | tf_op jit(solution)/shard_map/ppermute | solution.py:230
  10.0 0.8 %collective-permute-start.2 = (bf16[16,128]{1,0:T(8,128)(2,1)S(1)}, bf16[16,128]{1,0:T(8,128)(2,1)S(1)}, u32[]{:S(2)}, u32[]{:S(2)}) collective-permute-start(bf16[16,128]{1,0:T(8,128)(2,1)S(1)} %notes.1.refs_0_), channel_id=1, source_target_pairs={{0,4},{1,5},{2,6},{3,7},{4,0},{5,1},{6,2},{7,3},{8,12},{9,13},{10,... | collective-permute-start | bytes 12296 | tf_op jit(solution)/shard_map/ppermute | solution.py:230
  10.8 1.6 %collective-permute-start.1 = (bf16[16,128]{1,0:T(8,128)(2,1)S(1)}, bf16[16,128]{1,0:T(8,128)(2,1)S(1)}, u32[]{:S(2)}, u32[]{:S(2)}) collective-permute-start(bf16[16,128]{1,0:T(8,128)(2,1)S(1)} %notes.1.refs_0_), channel_id=1, source_target_pairs={{0,2},{1,3},{2,4},{3,5},{4,6},{5,7},{6,0},{7,1},{8,10},{9,11},{10,... | collective-permute-start | bytes 12296 | tf_op jit(solution)/shard_map/ppermute | solution.py:230
  12.4 0.0 copy-done.2
  12.4 0.6 copy.9
  13.0 0.8 %turn.1.act_ref = bf16[16,512,128]{2,1,0:T(8,128)(2,1)S(1)} custom-call(bf16[16,68,512]{2,1,0:T(8,128)(2,1)S(1)} %bitcast.12), custom_call_target="tpu_custom_call" | custom-call | tf_op jit(solution)/shard_map/turn/pallas_call | solution.py:209
  13.8 1.6 %collective-permute-done.4.refs_0_ = bf16[128,1792]{1,0:T(8,128)(2,1)S(1)} collective-permute-done((bf16[128,1792]{1,0:T(8,128)(2,1)S(1)}, bf16[128,1792]{1,0:T(8,128)(2,1)S(1)}, u32[]{:S(2)}, u32[]{:S(2)}) %collective-permute-start.4) | collective-permute-done | bytes 458784 | tf_op jit(solution)/shard_map/ppermute | solution.py:230
  15.3 1.2 %collective-permute-start.5 = (bf16[128,1792]{1,0:T(8,128)(2,1)S(1)}, bf16[128,1792]{1,0:T(8,128)(2,1)S(1)}, u32[]{:S(2)}, u32[]{:S(2)}) collective-permute-start(bf16[128,1792]{1,0:T(8,128)(2,1)S(1)} %collective-permute-done.4.refs_0_), channel_id=1, source_target_pairs={{0,2},{1,3},{2,4},{3,5},{4,6},{5,7},{6,0},{7,1},{8,10},{9,11},{10,... | collective-permute-start | bytes 1376264 | tf_op jit(solution)/shard_map/ppermute | solution.py:230
  16.5 0.0 collective-permute-done.3.refs_3_
  16.5 0.8 %collective-permute-done.2.refs_2_ = bf16[16,128]{1,0:T(8,128)(2,1)S(1)} collective-permute-done((bf16[16,128]{1,0:T(8,128)(2,1)S(1)}, bf16[16,128]{1,0:T(8,128)(2,1)S(1)}, u32[]{:S(2)}, u32[]{:S(2)}) %collective-permute-start.2) | collective-permute-done | bytes 4128 | tf_op jit(solution)/shard_map/ppermute | solution.py:230
  17.3 0.0 collective-permute-done.1.refs_1_
  17.3 0.0 collective-permute-done.refs_0_
  17.3 2.0 %collective-permute-start.7 = (bf16[128,1792]{1,0:T(8,128)(2,1)S(1)}, bf16[128,1792]{1,0:T(8,128)(2,1)S(1)}, u32[]{:S(2)}, u32[]{:S(2)}) collective-permute-start(bf16[128,1792]{1,0:T(8,128)(2,1)S(1)} %collective-permute-done.4.refs_0_), channel_id=1, source_target_pairs={{0,1},{1,0},{2,3},{3,2},{4,5},{5,4},{6,7},{7,6},{8,9},{9,8},{10,11... | collective-permute-start | bytes 1376264 | tf_op jit(solution)/shard_map/ppermute | solution.py:230
  19.3 4.2 %collective-permute-start.6 = (bf16[128,1792]{1,0:T(8,128)(2,1)S(1)}, bf16[128,1792]{1,0:T(8,128)(2,1)S(1)}, u32[]{:S(2)}, u32[]{:S(2)}) collective-permute-start(bf16[128,1792]{1,0:T(8,128)(2,1)S(1)} %bitcast_select_fusion), channel_id=1, source_target_pairs={{0,30},{1,31},{2,24},{3,25},{4,26},{5,27},{6,28},{7,29},{8,6},{9,7... | collective-permute-start | bytes 1376264 | tf_op jit(solution)/shard_map/ppermute | solution.py:230
  23.5 0.3 collective-permute-start.10
  23.8 0.7 %place.1.place_ref = bf16[4,272,128]{2,1,0:T(8,128)(2,1)S(1)} custom-call(bf16[16,128]{1,0:T(8,128)(2,1)S(1)} %notes.1.refs_0_, bf16[16,128]{1,0:T(8,128)(2,1)S(1)} %collective-permute-done.1.refs_1_, bf16[16,128]{1,0:T(8,128)(2,1)S(1)} %collective-permute-done.2.refs_2_, bf16[16,128]{1,0:T(8,128)(2,1)S(1)} %collective-permute-done.3.refs_3_), custom_call_target="tpu_custom_call" | custom-call | tf_op jit(solution)/shard_map/place/pallas_call | solution.py:209
  24.5 0.6 early.2.refs_0_
  25.1 3.5 %collective-permute-done.5.refs_1_ = bf16[128,1792]{1,0:T(8,128)(2,1)S(1)} collective-permute-done((bf16[128,1792]{1,0:T(8,128)(2,1)S(1)}, bf16[128,1792]{1,0:T(8,128)(2,1)S(1)}, u32[]{:S(2)}, u32[]{:S(2)}) %collective-permute-start.5) | collective-permute-done | bytes 458784 | tf_op jit(solution)/shard_map/ppermute | solution.py:230
  28.6 4.3 %collective-permute-start.8 = (bf16[128,1792]{1,0:T(8,128)(2,1)S(1)}, bf16[128,1792]{1,0:T(8,128)(2,1)S(1)}, u32[]{:S(2)}, u32[]{:S(2)}) collective-permute-start(bf16[128,1792]{1,0:T(8,128)(2,1)S(1)} %collective-permute-done.5.refs_1_), channel_id=1, source_target_pairs={{0,1},{1,0},{2,3},{3,2},{4,5},{5,4},{6,7},{7,6},{8,9},{9,8},{10,11... | collective-permute-start | bytes 1376264 | tf_op jit(solution)/shard_map/ppermute | solution.py:230
  32.9 0.9 %early.3 = (bf16[272,1792]{1,0:T(8,128)(2,1)S(1)}, bf16[272,1792]{1,0:T(8,128)(2,1)S(1)}) custom-call(bf16[4,272,128]{2,1,0:T(8,128)(2,1)S(1)} %place.1.place_ref, bf16[128,1792]{1,0:T(8,128)(2,1)S(1)} %collective-permute-done.4.refs_0_, bf16[128,1792]{1,0:T(8,128)(2,1)S(1)} %collective-permute-done.5.refs_1_), custom_call_target="tpu_custom_call" | custom-call | tf_op jit(solution)/shard_map/early/pallas_call | solution.py:209
  33.8 0.0 collective-permute-done.7.refs_1_
  33.8 6.4 %collective-permute-done.6.refs_3_ = bf16[128,1792]{1,0:T(8,128)(2,1)S(1)} collective-permute-done((bf16[128,1792]{1,0:T(8,128)(2,1)S(1)}, bf16[128,1792]{1,0:T(8,128)(2,1)S(1)}, u32[]{:S(2)}, u32[]{:S(2)}) %collective-permute-start.6) | collective-permute-done | bytes 458784 | tf_op jit(solution)/shard_map/ppermute | solution.py:230
  40.3 0.3 collective-permute-start.9
  40.5 0.0 collective-permute-done.10.refs_0_
  40.5 12.2 %weight_grad.2.refs_4_ = bf16[16,512,3584]{2,1,0:T(8,128)(2,1)} custom-call(bf16[4,272,128]{2,1,0:T(8,128)(2,1)S(1)} %place.1.place_ref, bf16[16,512,128]{2,1,0:T(8,128)(2,1)S(1)} %turn.1.act_ref, bf16[128,1792]{1,0:T(8,128)(2,1)S(1)} %collective-permute-done.10.refs_0_, bf16[272,1792]{1,0:T(8,128)(2,1)S(1)} %get-tuple-element.31.refs_1_, ...), custom_call_target="tpu_custom_call" | custom-call | flops 7516192768 | bytes 29360128 | tf_op jit(solution)/shard_map/weight_grad/pallas_call | solution.py:240
  52.8 0.0 collective-permute-done.8.refs_2_
  52.8 0.8 %collective-permute-done.9.refs_3_ = bf16[128,1792]{1,0:T(8,128)(2,1)S(1)} collective-permute-done((bf16[128,1792]{1,0:T(8,128)(2,1)S(1)}, bf16[128,1792]{1,0:T(8,128)(2,1)S(1)}, u32[]{:S(2)}, u32[]{:S(2)}) %collective-permute-start.9) | collective-permute-done | bytes 458784 | tf_op jit(solution)/shard_map/ppermute | solution.py:230
  53.6 12.5 %weight_grad.3 = bf16[16,512,3584]{2,1,0:T(8,128)(2,1)} custom-call(bf16[4,272,128]{2,1,0:T(8,128)(2,1)S(1)} %place.1.place_ref, bf16[16,512,128]{2,1,0:T(8,128)(2,1)S(1)} %turn.1.act_ref, bf16[272,1792]{1,0:T(8,128)(2,1)S(1)} %early.2.refs_0_, bf16[128,1792]{1,0:T(8,128)(2,1)S(1)} %collective-permute-done.7.refs_1_, ...), custom_call_target="tpu_custom_call", output_to_operand_aliasing={{}: (6, {})} | custom-call | flops 7516192768 | bytes 29360128 | tf_op jit(solution)/shard_map/weight_grad/pallas_call | solution.py:240
  (1 shorter events, 0.0 us)
Async XLA Ops:
  0.0 12.4 %copy-start.2 = (bf16[1,16,68,512]{3,1,2,0:T(8,128)(2,1)S(1)}, bf16[1,16,68,512]{3,1,2,0:T(8,128)(2,1)}, u32[]{:S(2)}) copy-start(bf16[1,16,68,512]{3,1,2,0:T(8,128)(2,1)} %param.9) | copy-start | bytes 3342340
  1.3 14.0 %collective-permute-start.4 = (bf16[128,1792]{1,0:T(8,128)(2,1)S(1)}, bf16[128,1792]{1,0:T(8,128)(2,1)S(1)}, u32[]{:S(2)}, u32[]{:S(2)}) collective-permute-start(bf16[128,1792]{1,0:T(8,128)(2,1)S(1)} %bitcast_select_fusion), channel_id=1, source_target_pairs={{0,26},{1,27},{2,28},{3,29},{4,30},{5,31},{6,24},{7,25},{8,2},{9,3... | collective-permute-start | bytes 1376264 | tf_op jit(solution)/shard_map/ppermute | solution.py:230
  4.6 12.6 %collective-permute-start = (bf16[128,1792]{1,0:T(8,128)(2,1)S(1)}, bf16[128,1792]{1,0:T(8,128)(2,1)S(1)}, u32[]{:S(2)}, u32[]{:S(2)}) collective-permute-start(bf16[128,1792]{1,0:T(8,128)(2,1)S(1)} %bitcast_select_fusion), channel_id=1, source_target_pairs={{0,25},{1,24},{2,27},{3,26},{4,29},{5,28},{6,31},{7,30},{8,1},{9,0... | collective-permute-start | bytes 1376264 | tf_op jit(solution)/shard_map/ppermute | solution.py:230
  6.4 0.7 %copy-start = (s32[1,128,8]{1,2,0:T(8,128)S(1)}, s32[1,128,8]{1,2,0:T(8,128)}, u32[]{:S(2)}) copy-start(s32[1,128,8]{1,2,0:T(8,128)} %param.8) | copy-start | bytes 12292
  7.1 0.7 %copy-start.1 = (bf16[1,128,8]{1,2,0:T(8,128)(2,1)S(1)}, bf16[1,128,8]{1,2,0:T(8,128)(2,1)}, u32[]{:S(2)}) copy-start(bf16[1,128,8]{1,2,0:T(8,128)(2,1)} %param.7) | copy-start | bytes 6148
  7.8 8.7 %collective-permute-start.3 = (bf16[16,128]{1,0:T(8,128)(2,1)S(1)}, bf16[16,128]{1,0:T(8,128)(2,1)S(1)}, u32[]{:S(2)}, u32[]{:S(2)}) collective-permute-start(bf16[16,128]{1,0:T(8,128)(2,1)S(1)} %notes.1.refs_0_), channel_id=1, source_target_pairs={{0,6},{1,7},{2,0},{3,1},{4,2},{5,3},{6,4},{7,5},{8,14},{9,15},{10,... | collective-permute-start | bytes 12296 | tf_op jit(solution)/shard_map/ppermute | solution.py:230
  10.0 7.2 %collective-permute-start.2 = (bf16[16,128]{1,0:T(8,128)(2,1)S(1)}, bf16[16,128]{1,0:T(8,128)(2,1)S(1)}, u32[]{:S(2)}, u32[]{:S(2)}) collective-permute-start(bf16[16,128]{1,0:T(8,128)(2,1)S(1)} %notes.1.refs_0_), channel_id=1, source_target_pairs={{0,4},{1,5},{2,6},{3,7},{4,0},{5,1},{6,2},{7,3},{8,12},{9,13},{10,... | collective-permute-start | bytes 12296 | tf_op jit(solution)/shard_map/ppermute | solution.py:230
  10.8 6.5 %collective-permute-start.1 = (bf16[16,128]{1,0:T(8,128)(2,1)S(1)}, bf16[16,128]{1,0:T(8,128)(2,1)S(1)}, u32[]{:S(2)}, u32[]{:S(2)}) collective-permute-start(bf16[16,128]{1,0:T(8,128)(2,1)S(1)} %notes.1.refs_0_), channel_id=1, source_target_pairs={{0,2},{1,3},{2,4},{3,5},{4,6},{5,7},{6,0},{7,1},{8,10},{9,11},{10,... | collective-permute-start | bytes 12296 | tf_op jit(solution)/shard_map/ppermute | solution.py:230
  15.3 13.2 %collective-permute-start.5 = (bf16[128,1792]{1,0:T(8,128)(2,1)S(1)}, bf16[128,1792]{1,0:T(8,128)(2,1)S(1)}, u32[]{:S(2)}, u32[]{:S(2)}) collective-permute-start(bf16[128,1792]{1,0:T(8,128)(2,1)S(1)} %collective-permute-done.4.refs_0_), channel_id=1, source_target_pairs={{0,2},{1,3},{2,4},{3,5},{4,6},{5,7},{6,0},{7,1},{8,10},{9,11},{10,... | collective-permute-start | bytes 1376264 | tf_op jit(solution)/shard_map/ppermute | solution.py:230
  17.3 16.5 %collective-permute-start.7 = (bf16[128,1792]{1,0:T(8,128)(2,1)S(1)}, bf16[128,1792]{1,0:T(8,128)(2,1)S(1)}, u32[]{:S(2)}, u32[]{:S(2)}) collective-permute-start(bf16[128,1792]{1,0:T(8,128)(2,1)S(1)} %collective-permute-done.4.refs_0_), channel_id=1, source_target_pairs={{0,1},{1,0},{2,3},{3,2},{4,5},{5,4},{6,7},{7,6},{8,9},{9,8},{10,11... | collective-permute-start | bytes 1376264 | tf_op jit(solution)/shard_map/ppermute | solution.py:230
  19.3 21.0 %collective-permute-start.6 = (bf16[128,1792]{1,0:T(8,128)(2,1)S(1)}, bf16[128,1792]{1,0:T(8,128)(2,1)S(1)}, u32[]{:S(2)}, u32[]{:S(2)}) collective-permute-start(bf16[128,1792]{1,0:T(8,128)(2,1)S(1)} %bitcast_select_fusion), channel_id=1, source_target_pairs={{0,30},{1,31},{2,24},{3,25},{4,26},{5,27},{6,28},{7,29},{8,6},{9,7... | collective-permute-start | bytes 1376264 | tf_op jit(solution)/shard_map/ppermute | solution.py:230
  23.5 17.1 %collective-permute-start.10 = (bf16[128,1792]{1,0:T(8,128)(2,1)S(1)}, bf16[128,1792]{1,0:T(8,128)(2,1)S(1)}, u32[]{:S(2)}, u32[]{:S(2)}) collective-permute-start(bf16[128,1792]{1,0:T(8,128)(2,1)S(1)} %bitcast_select_fusion), channel_id=1, source_target_pairs={{0,24},{1,25},{2,26},{3,27},{4,28},{5,29},{6,30},{7,31},{8,0},{9,1... | collective-permute-start | bytes 1376264 | tf_op jit(solution)/shard_map/ppermute | solution.py:230
  28.6 24.2 %collective-permute-start.8 = (bf16[128,1792]{1,0:T(8,128)(2,1)S(1)}, bf16[128,1792]{1,0:T(8,128)(2,1)S(1)}, u32[]{:S(2)}, u32[]{:S(2)}) collective-permute-start(bf16[128,1792]{1,0:T(8,128)(2,1)S(1)} %collective-permute-done.5.refs_1_), channel_id=1, source_target_pairs={{0,1},{1,0},{2,3},{3,2},{4,5},{5,4},{6,7},{7,6},{8,9},{9,8},{10,11... | collective-permute-start | bytes 1376264 | tf_op jit(solution)/shard_map/ppermute | solution.py:230
  40.3 13.4 %collective-permute-start.9 = (bf16[128,1792]{1,0:T(8,128)(2,1)S(1)}, bf16[128,1792]{1,0:T(8,128)(2,1)S(1)}, u32[]{:S(2)}, u32[]{:S(2)}) collective-permute-start(bf16[128,1792]{1,0:T(8,128)(2,1)S(1)} %collective-permute-done.6.refs_3_), channel_id=1, source_target_pairs={{0,1},{1,0},{2,3},{3,2},{4,5},{5,4},{6,7},{7,6},{8,9},{9,8},{10,11... | collective-permute-start | bytes 1376264 | tf_op jit(solution)/shard_map/ppermute | solution.py:230
